TPU v7x, 32 devices: a whole 2x2x4 slice. The times are simulated.
32 devices in a mesh: graph: 2 (over core), dom: 16 (over z, y, x).
Axes of the slice: x: 2, y: 2, z: 4, core: 2. Of those that a mesh axis runs over, the one named last changes fastest.
Arguments:
- embeddings: float32 [2, 8192, 300], P('graph', 'dom'), may hold values from -6 to 6
- first_weight: float32 [300, 300], replicated, may hold values from -0.375 to 0.375
- second_weight: float32 [300, 300], replicated, may hold values from -0.375 to 0.375
- bound_index: int32 [2, 16, 2, 64], P('graph', 'dom'), may hold values from 0 to 511
- neighbors: int32 [2, 8192, 16], P('graph', 'dom'), may hold values from 0 to 639
- degree: int32 [2, 8192], P('graph', 'dom'), may hold values from 1 to 16
- send_index: int32 [2, 16, 32, 32], P('graph', 'dom'), may hold values from 0 to 512, as said below
- recv_count: int32 [2, 16, 32], P('graph', 'dom'), may hold values from 8 to 32, as said below
- pair_index: int32 [2, 16, 2, 128], P('graph', 'dom'), may hold values from 0 to 1023, as said below
Outputs:
- grad_embeddings: float32 [2, 8192, 300], P('graph', 'dom')
- grad_first: float32 [300, 300], replicated
- grad_second: float32 [300, 300], replicated
- cluster_loss: float32 [2, 16], P('graph', 'dom')
Inputs may be any that keep to these rules, and one draw needn't show every extreme that they name: `send_index`: for each sending partition and owner, filled slots come first and hold local rows, the empty ones hold 512; every local row is sent exactly once; in each aligned group of four owners one receives 32 rows from every partition. `recv_count`: equals the number of filled slots that send_index gives for this owner and that partition. `pair_index`: entries are s * 32 + c. Side 0 names each of the first 8 slots of every graph-0 partition once, side 1 each of the first 8 slots of every graph-1 partition once.
All inputs are finite; a program needn't handle non-finite values.
Results may differ from a plain program's by a relative error of at most 0.0003.
Values sent between devices are 32-bit elements; how exact they have to be, the bound alone decides.
A program may use at most 64 MiB of HBM per device.

v0:
```python
import math

import jax
import jax.numpy as jnp
from jax import lax
from jax.sharding import PartitionSpec as P

SOFTMAX_HEAT = 0.02
EPSILON = 1e-06
TOP_PRECISION = lax.Precision.HIGHEST


def with_halo(cells, sides, width):
    for axis, dim in sides:
        count = lax.axis_size(axis)
        head = lax.slice_in_dim(cells, 0, width, axis=dim)
        tail = lax.slice_in_dim(cells, cells.shape[dim] - width, cells.shape[dim], axis=dim)
        cells = jnp.concatenate(
            [
                lax.ppermute(tail, axis, [(i, (i + 1) % count) for i in range(count)]),
                cells,
                lax.ppermute(head, axis, [((i + 1) % count, i) for i in range(count)]),
            ],
            axis=dim,
        )
    return cells


def count_matrix(pool_rows, neighbor_ids, degree_row):
    row_count = neighbor_ids.shape[0]
    rim_width = (pool_rows - row_count) // 2
    columns = jnp.arange(pool_rows, dtype=jnp.int32)
    slot_ids = jnp.arange(neighbor_ids.shape[1], dtype=jnp.int32)
    live_mask = slot_ids[None, :] < degree_row[:, None]
    hits = (neighbor_ids[:, :, None] == columns[None, None, :]) & live_mask[:, :, None]
    counts = jnp.sum(hits.astype(jnp.float32), axis=1)
    self_rows = jnp.arange(row_count, dtype=jnp.int32) + rim_width
    return counts + (columns[None, :] == self_rows[:, None]).astype(jnp.float32)


def aggregate(counts, pool, degree_row):
    summed = jnp.dot(counts, pool, precision=TOP_PRECISION, preferred_element_type=jnp.float32)
    return summed / (1.0 + degree_row.astype(jnp.float32))[:, None]


def cluster_term(incoming_rows, counts, pair_rows):
    slot_total = incoming_rows.shape[0]
    slot_cap = slot_total // counts.shape[0]
    live_mask = (jnp.arange(slot_cap, dtype=jnp.int32)[None, :] < counts[:, None]).reshape(
        slot_total
    )
    half_slot_count = slot_total // 2
    source_entity = incoming_rows[pair_rows[0]]
    target_entity = incoming_rows[pair_rows[1]]
    first_layer_logits = (
        jnp.dot(
            source_entity,
            incoming_rows[half_slot_count:].T,
            precision=TOP_PRECISION,
            preferred_element_type=jnp.float32,
        )
        / SOFTMAX_HEAT
    )
    second_layer_logits = (
        jnp.dot(
            target_entity,
            incoming_rows[:half_slot_count].T,
            precision=TOP_PRECISION,
            preferred_element_type=jnp.float32,
        )
        / SOFTMAX_HEAT
    )
    first_total = jnp.log(
        jnp.sum(
            jnp.where(live_mask[half_slot_count:][None, :], jnp.exp(first_layer_logits), 0.0),
            axis=1,
        )
    )
    second_total = jnp.log(
        jnp.sum(
            jnp.where(live_mask[:half_slot_count][None, :], jnp.exp(second_layer_logits), 0.0),
            axis=1,
        )
    )
    positive_match = jnp.sum(source_entity * target_entity, axis=1) / SOFTMAX_HEAT
    return jnp.sum(first_total + second_total - 2.0 * positive_match)


def on_device(
    embeddings,
    first_weight,
    second_weight,
    bound_index,
    neighbors,
    degree,
    send_index,
    recv_count,
    pair_index,
):
    inputs = embeddings[0]
    row_count, feat_width = inputs.shape
    rim_width = bound_index.shape[-1]
    lower_rows = bound_index[0, 0, 0]
    upper_rows = bound_index[0, 0, 1]
    neighbor_ids = neighbors[0]
    degree_row = degree[0]
    graph_count = lax.axis_size("graph")
    domain_count = lax.axis_size("dom")
    devices = graph_count * domain_count
    routes = send_index[0, 0]
    slot_cap = routes.shape[1]
    pair_count = pair_index.shape[-1]
    adjacency = count_matrix(row_count + 2 * rim_width, neighbor_ids, degree_row)

    def fetch(table):
        edge_rows = jnp.concatenate([table[lower_rows], table[upper_rows]], axis=0)
        extended = with_halo(edge_rows, (("dom", 0),), rim_width)
        return jnp.concatenate([extended[:rim_width], table, extended[-rim_width:]], axis=0)

    def return_rim(grad_pool):
        center = grad_pool[rim_width : rim_width + row_count]
        edge_rows = jnp.concatenate([grad_pool[:rim_width], grad_pool[-rim_width:]], axis=0)
        extended = with_halo(edge_rows, (("dom", 0),), rim_width)
        center = center.at[lower_rows].add(extended[:rim_width])
        return center.at[upper_rows].add(extended[-rim_width:])

    def spread(pool):
        return aggregate(adjacency, pool, degree_row)

    def loss_of(incoming_rows):
        return cluster_term(incoming_rows, recv_count[0, 0], pair_index[0, 0])

    pool_one = fetch(inputs)
    mixed_one, back_one = jax.vjp(spread, pool_one)
    hidden = jnp.tanh(
        jnp.dot(
            mixed_one, first_weight, precision=TOP_PRECISION, preferred_element_type=jnp.float32
        )
    )
    pool_two = fetch(hidden)
    mixed_two, back_two = jax.vjp(spread, pool_two)
    latent = jnp.dot(
        mixed_two, second_weight, precision=TOP_PRECISION, preferred_element_type=jnp.float32
    )
    length = jnp.sqrt(jnp.sum(latent * latent, axis=1, keepdims=True) + EPSILON)
    unit_rows = latent / length
    padded = jnp.concatenate([unit_rows, jnp.zeros((1, feat_width), jnp.float32)], axis=0)
    outgoing = padded[routes]
    arrived = lax.all_to_all(outgoing, ("graph", "dom"), split_axis=0, concat_axis=0, tiled=True)
    arrived = arrived.reshape(devices * slot_cap, feat_width)
    cluster_value, cluster_back = jax.vjp(loss_of, arrived)
    (grad_arrived,) = cluster_back(jnp.ones((), jnp.float32))
    returned = lax.all_to_all(
        grad_arrived.reshape(devices, slot_cap, feat_width),
        ("graph", "dom"),
        split_axis=0,
        concat_axis=0,
        tiled=True,
    )
    grad_unit = (
        jnp.zeros((row_count + 1, feat_width), jnp.float32).at[routes].add(returned)[:row_count]
    )
    grad_latent = (
        grad_unit - unit_rows * jnp.sum(grad_unit * unit_rows, axis=1, keepdims=True)
    ) / length
    grad_second = jnp.dot(
        mixed_two.T, grad_latent, precision=TOP_PRECISION, preferred_element_type=jnp.float32
    )
    grad_mixed_two = jnp.dot(
        grad_latent, second_weight.T, precision=TOP_PRECISION, preferred_element_type=jnp.float32
    )
    (grad_pool_two,) = back_two(grad_mixed_two)
    grad_hidden = return_rim(grad_pool_two)
    grad_inner = grad_hidden * (1.0 - hidden * hidden)
    grad_first = jnp.dot(
        mixed_one.T, grad_inner, precision=TOP_PRECISION, preferred_element_type=jnp.float32
    )
    grad_mixed_one = jnp.dot(
        grad_inner, first_weight.T, precision=TOP_PRECISION, preferred_element_type=jnp.float32
    )
    (grad_pool_one,) = back_one(grad_mixed_one)
    grad_inputs = return_rim(grad_pool_one)
    grad_first, grad_second = lax.psum((grad_first, grad_second), ("graph", "dom"))
    grad_scale = 1.0 / math.sqrt(row_count * devices)
    cluster_mean = (cluster_value / (2.0 * pair_count)).reshape(1, 1)
    return (grad_inputs[None], grad_first * grad_scale, grad_second * grad_scale, cluster_mean)


def solution(mesh):
    in_specs = (
        P("graph", "dom", None),
        P(),
        P(),
        P("graph", "dom", None, None),
        P("graph", "dom", None),
        P("graph", "dom"),
        P("graph", "dom", None, None),
        P("graph", "dom", None),
        P("graph", "dom", None, None),
    )
    out_specs = (P("graph", "dom", None), P(), P(), P("graph", "dom"))
    return jax.shard_map(
        on_device, mesh=mesh, in_specs=in_specs, out_specs=out_specs, check_vma=False
    )
```

profile of v0, /device:TPU:0, one launch (start us, length us, event | category | flops | bytes accessed | tf_op | source)
XLA Modules:
  0.0 331.2 jit_solution(15527398296197626989)
XLA Ops:
  10.5 3.0 collective-permute-start
  14.2 4.1 %collective-permute-start.1 = (f32[64,300]{1,0:T(8,128)S(1)}, f32[64,300]{1,0:T(8,128)S(1)}, u32[]{:S(2)}, u32[]{:S(2)}) collective-permute-start(f32[64,300]{1,0:T(8,128)S(1)} %gather_fusion.1), channel_id=1, source_target_pairs={{1,0},{2,1},{3,2},{4,3},{5,4},{6,5},{7,6},{8,7},{9,8},{10,9},{11,1... | collective-permute-start | bytes 230408 | tf_op jit(solution)/shard_map/ppermute | solution.py:22
  18.6 6.2 %convert_reduce_fusion = f32[512,640]{1,0:T(8,128)S(1)} fusion(s32[512,16]{1,0:T(8,128)S(1)} %copy.43, pred[512,16]{1,0:T(8,128)(4,1)S(1)} %iota_compare_fusion.2), kind=kLoop, calls=%fused_computation.13 | loop fusion | flops 20643840 | bytes 1351680 | tf_op jit(solution)/shard_map/reduce_sum | solution.py:36
  24.9 2.2 convolution_divide_fusion.2
  31.0 5.7 %collective-permute-start.3 = (f32[64,300]{0,1:T(8,128)S(1)}, f32[64,300]{0,1:T(8,128)S(1)}, u32[]{:S(2)}, u32[]{:S(2)}) collective-permute-start(f32[64,300]{0,1:T(8,128)S(1)} %copy.48), channel_id=1, source_target_pairs={{1,0},{2,1},{3,2},{4,3},{5,4},{6,5},{7,6},{8,7},{9,8},{10,9},{11,1... | collective-permute-start | bytes 230408 | tf_op jit(solution)/shard_map/ppermute | solution.py:22
  36.7 3.3 collective-permute-done.2
  40.0 2.0 convolution_divide_fusion.3
  44.5 4.8 %gather_fusion.4 = f32[1024,300]{1,0:T(8,128)} fusion(f32[513,300]{1,0:T(8,128)S(1)} %concatenate.17.clone, s32[1024]{0:T(1024)S(1)} %broadcast_clamp_fusion), kind=kCustom, calls=%fused_computation.4 | custom fusion | bytes 2461696 | tf_op jit(solution)/shard_map/gather | solution.py:148
  49.4 5.9 %all-to-all-start = ((f32[32,32,300]{2,1,0:T(8,128)}), f32[32,32,300]{2,1,0:T(8,128)S(1)}, u32[]{:S(2)}, u32[]{:S(2)}) async-start(f32[32,32,300]{2,1,0:T(8,128)} %bitcast.60), calls=%async_computation | async-start | bytes 3145728 | tf_op jit(solution)/shard_map/all_to_all | solution.py:149
  58.0 36.7 %all-to-all-done = f32[32,32,300]{2,1,0:T(8,128)S(1)} async-done(((f32[32,32,300]{2,1,0:T(8,128)}), f32[32,32,300]{2,1,0:T(8,128)S(1)}, u32[]{:S(2)}, u32[]{:S(2)}) %all-to-all-start) | async-done | bytes 1228832 | tf_op jit(solution)/shard_map/all_to_all | solution.py:149
  111.2 1.8 copy.52
  113.0 3.1 scatter_fusion
  116.1 41.7 %all_to_all.10 = f32[32,32,300]{2,1,0:T(8,128)} all-to-all(f32[32,32,300]{2,1,0:T(8,128)S(1)} %bitcast.49), channel_id=1, replica_groups=mesh['graph'=2,'dom'=16] {'graph','dom'}, dimensions={0} | all-to-all | bytes 2457600 | tf_op jit(solution)/shard_map/all_to_all | solution.py:153
  157.8 7.7 %scatter_custom_fusion.1 = f32[513,300]{1,0:T(8,128)S(1)} fusion(s32[1024]{0:T(1024)} %copy-done.15, f32[1024,300]{1,0:T(8,128)} %bitcast.61, f32[]{:T(128)} %constant.13.clone.1), kind=kCustom, calls=%fused_computation.50 | custom fusion | flops 307200 | bytes 616112 | tf_op jit(solution)/shard_map/scatter-add | solution.py:161
  169.4 2.0 fusion.9
  171.5 5.6 %collective-permute-start.5 = (f32[64,300]{0,1:T(8,128)S(1)}, f32[64,300]{0,1:T(8,128)}, u32[]{:S(2)}, u32[]{:S(2)}) collective-permute-start(f32[64,300]{0,1:T(8,128)S(1)} %get-tuple-element.22), channel_id=1, source_target_pairs={{1,0},{2,1},{3,2},{4,3},{5,4},{6,5},{7,6},{8,7},{9,8},{10,9},{11,1... | collective-permute-start | bytes 230408 | tf_op jit(solution)/shard_map/ppermute | solution.py:22
  177.2 2.0 fusion.54
  186.4 3.3 fusion.23
  189.7 3.1 convolution_divide_fusion
  193.8 2.0 fusion.8
  196.0 5.6 %collective-permute-start.7 = (f32[64,300]{0,1:T(8,128)S(1)}, f32[64,300]{0,1:T(8,128)S(1)}, u32[]{:S(2)}, u32[]{:S(2)}) collective-permute-start(f32[64,300]{0,1:T(8,128)S(1)} %get-tuple-element.20), channel_id=1, source_target_pairs={{1,0},{2,1},{3,2},{4,3},{5,4},{6,5},{7,6},{8,7},{9,8},{10,9},{11,1... | collective-permute-start | bytes 230408 | tf_op jit(solution)/shard_map/ppermute | solution.py:22
  202.7 2.9 collective-permute-done.6
  209.5 111.5 %all-reduce.6.cloned.1.call-done = (f32[300,300]{1,0:T(8,128)}, f32[300,300]{1,0:T(8,128)}) async-done(((f32[300,300]{1,0:T(8,128)}, f32[300,300]{1,0:T(8,128)}), (f32[300,300]{1,0:T(8,128)}, f32[300,300]{1,0:T(8,128)})) %all-reduce.6.cloned.1.call-update) | async-done | bytes 720016 | tf_op jit(solution)/shard_map/psum | solution.py:183
  321.0 2.1 broadcast_multiply_fusion
  (139 shorter events, 46.6 us)
Async XLA Ops:
  7.2 34.9 %copy-start = (f32[300,300]{1,0:T(8,128)S(1)}, f32[300,300]{1,0:T(8,128)}, u32[]{:S(2)}) copy-start(f32[300,300]{1,0:T(8,128)} %param.11) | copy-start | bytes 1080004
  7.9 6.2 %copy-start.21 = (s32[64]{0:T(128)}, s32[64]{0:T(128)S(1)}, u32[]{:S(2)}) copy-start(s32[64]{0:T(128)S(1)} %get-tuple-element.29) | copy-start | bytes 772
  8.4 9.8 %copy-start.23 = (s32[1,512]{1,0:T(1,128)S(1)}, s32[1,512]{1,0:T(1,128)}, u32[]{:S(2)}) copy-start(s32[1,512]{1,0:T(1,128)} %param.14) | copy-start | bytes 6148
  8.5 9.9 %copy-start.14 = (s32[1,512,16]{1,2,0:T(8,128)S(1)}, s32[1,512,16]{1,2,0:T(8,128)}, u32[]{:S(2)}) copy-start(s32[1,512,16]{1,2,0:T(8,128)} %param.13) | copy-start | bytes 98308
  9.8 8.7 %copy-start.16 = (s32[1,1,32,32]{3,2,1,0:T(8,128)S(1)}, s32[1,1,32,32]{3,2,1,0:T(8,128)}, u32[]{:S(2)}) copy-start(s32[1,1,32,32]{3,2,1,0:T(8,128)} %param.15) | copy-start | bytes 12292
  10.5 14.4 %collective-permute-start = (f32[64,300]{1,0:T(8,128)S(1)}, f32[64,300]{1,0:T(8,128)S(1)}, u32[]{:S(2)}, u32[]{:S(2)}) collective-permute-start(f32[64,300]{1,0:T(8,128)S(1)} %gather_fusion), channel_id=1, source_target_pairs={{0,1},{1,2},{2,3},{3,4},{4,5},{5,6},{6,7},{7,8},{8,9},{9,10},{10,1... | collective-permute-start | bytes 230408 | tf_op jit(solution)/shard_map/ppermute | solution.py:20
  14.2 10.7 %collective-permute-start.1 = (f32[64,300]{1,0:T(8,128)S(1)}, f32[64,300]{1,0:T(8,128)S(1)}, u32[]{:S(2)}, u32[]{:S(2)}) collective-permute-start(f32[64,300]{1,0:T(8,128)S(1)} %gather_fusion.1), channel_id=1, source_target_pairs={{1,0},{2,1},{3,2},{4,3},{5,4},{6,5},{7,6},{8,7},{9,8},{10,9},{11,1... | collective-permute-start | bytes 230408 | tf_op jit(solution)/shard_map/ppermute | solution.py:22
  18.4 21.6 %copy-start.26 = (f32[512]{0:T(512)}, f32[512]{0:T(512)S(1)}, u32[]{:S(2)}) copy-start(f32[512]{0:T(512)S(1)} %convert_add_fusion.5) | copy-start | bytes 6148
  18.6 18.1 %copy-start.15 = (s32[1024]{0:T(1024)}, s32[1024]{0:T(1024)S(1)}, u32[]{:S(2)}) copy-start(s32[1024]{0:T(1024)S(1)} %reshape.282) | copy-start | bytes 12292
  24.8 3.1 copy-start.13
  29.2 10.9 %copy-start.3 = (f32[512,300]{0,1:T(8,128)}, f32[512,300]{0,1:T(8,128)S(1)}, u32[]{:S(2)}) copy-start(f32[512,300]{0,1:T(8,128)S(1)} %convolution_tanh_fusion) | copy-start | bytes 1843204
  30.9 9.1 %collective-permute-start.2 = (f32[64,300]{0,1:T(8,128)S(1)}, f32[64,300]{0,1:T(8,128)S(1)}, u32[]{:S(2)}, u32[]{:S(2)}) collective-permute-start(f32[64,300]{0,1:T(8,128)S(1)} %copy.46), channel_id=1, source_target_pairs={{0,1},{1,2},{2,3},{3,4},{4,5},{5,6},{6,7},{7,8},{8,9},{9,10},{10,1... | collective-permute-start | bytes 230408 | tf_op jit(solution)/shard_map/ppermute | solution.py:20
  31.0 9.0 %collective-permute-start.3 = (f32[64,300]{0,1:T(8,128)S(1)}, f32[64,300]{0,1:T(8,128)S(1)}, u32[]{:S(2)}, u32[]{:S(2)}) collective-permute-start(f32[64,300]{0,1:T(8,128)S(1)} %copy.48), channel_id=1, source_target_pairs={{1,0},{2,1},{3,2},{4,3},{5,4},{6,5},{7,6},{8,7},{9,8},{10,9},{11,1... | collective-permute-start | bytes 230408 | tf_op jit(solution)/shard_map/ppermute | solution.py:22
  49.4 6.1 %copy-start.29 = (s32[1,1,32]{2,1,0:T(1,128)S(1)}, s32[1,1,32]{2,1,0:T(1,128)}, u32[]{:S(2)}) copy-start(s32[1,1,32]{2,1,0:T(1,128)} %param.16) | copy-start | bytes 388
  49.4 7.4 %copy-start.28 = (s32[1,1,2,128]{3,2,1,0:T(2,128)S(1)}, s32[1,1,2,128]{3,2,1,0:T(2,128)}, u32[]{:S(2)}) copy-start(s32[1,1,2,128]{3,2,1,0:T(2,128)} %param.17) | copy-start | bytes 3076
  49.4 45.2 %all-to-all-start = ((f32[32,32,300]{2,1,0:T(8,128)}), f32[32,32,300]{2,1,0:T(8,128)S(1)}, u32[]{:S(2)}, u32[]{:S(2)}) async-start(f32[32,32,300]{2,1,0:T(8,128)} %bitcast.60), calls=%async_computation | async-start | bytes 3145728 | tf_op jit(solution)/shard_map/all_to_all | solution.py:149
  55.3 265.8 %all-reduce.6.cloned.1.call-start = ((), (), s32[]{:S(2)}) async-start(), calls=%async_computation.2 | async-start | bytes 1867776 | tf_op jit(solution)/shard_map/psum | solution.py:183
  169.4 7.8 %copy-start.9 = (f32[512,300]{0,1:T(8,128)S(1)}, f32[512,300]{0,1:T(8,128)}, u32[]{:S(2)}) copy-start(f32[512,300]{0,1:T(8,128)} %copy-done.8) | copy-start | bytes 1843204
  171.5 9.1 %collective-permute-start.4 = (f32[64,300]{0,1:T(8,128)S(1)}, f32[64,300]{0,1:T(8,128)}, u32[]{:S(2)}, u32[]{:S(2)}) collective-permute-start(f32[64,300]{0,1:T(8,128)S(1)} %get-tuple-element.23), channel_id=1, source_target_pairs={{0,1},{1,2},{2,3},{3,4},{4,5},{5,6},{6,7},{7,8},{8,9},{9,10},{10,1... | collective-permute-start | bytes 230408 | tf_op jit(solution)/shard_map/ppermute | solution.py:20
  171.5 11.4 %collective-permute-start.5 = (f32[64,300]{0,1:T(8,128)S(1)}, f32[64,300]{0,1:T(8,128)}, u32[]{:S(2)}, u32[]{:S(2)}) collective-permute-start(f32[64,300]{0,1:T(8,128)S(1)} %get-tuple-element.22), channel_id=1, source_target_pairs={{1,0},{2,1},{3,2},{4,3},{5,4},{6,5},{7,6},{8,7},{9,8},{10,9},{11,1... | collective-permute-start | bytes 230408 | tf_op jit(solution)/shard_map/ppermute | solution.py:22
  179.7 4.3 %copy-start.20 = (s32[64]{0:T(128)S(1)}, s32[64]{0:T(128)}, u32[]{:S(2)}) copy-start(s32[64]{0:T(128)} %copy-done.19) | copy-start | bytes 772
  186.3 3.3 copy-start.6
  195.9 9.7 %collective-permute-start.6 = (f32[64,300]{0,1:T(8,128)S(1)}, f32[64,300]{0,1:T(8,128)S(1)}, u32[]{:S(2)}, u32[]{:S(2)}) collective-permute-start(f32[64,300]{0,1:T(8,128)S(1)} %get-tuple-element.21), channel_id=1, source_target_pairs={{0,1},{1,2},{2,3},{3,4},{4,5},{5,6},{6,7},{7,8},{8,9},{9,10},{10,1... | collective-permute-start | bytes 230408 | tf_op jit(solution)/shard_map/ppermute | solution.py:20
  196.0 11.0 %collective-permute-start.7 = (f32[64,300]{0,1:T(8,128)S(1)}, f32[64,300]{0,1:T(8,128)S(1)}, u32[]{:S(2)}, u32[]{:S(2)}) collective-permute-start(f32[64,300]{0,1:T(8,128)S(1)} %get-tuple-element.20), channel_id=1, source_target_pairs={{1,0},{2,1},{3,2},{4,3},{5,4},{6,5},{7,6},{8,7},{9,8},{10,9},{11,1... | collective-permute-start | bytes 230408 | tf_op jit(solution)/shard_map/ppermute | solution.py:22
  (16 other events, 26.4 us)
Sparse Core Ops, SparseCore 0:
  192.9 128.1 all-reduce.5
where the time goes:
time: 332 us; the launch traced here: 331 us
  waiting for transfers between devices  155 us (47%)
  blocking collectives  41.7 us (13%)
  local copies, waits for them, and re-layouts  30.7 us (9%)
  starting transfers between devices  30.2 us (9%)
  other arithmetic  30.1 us (9%)
  matrix products  26.7 us (8%)
  between operations  16.4 us (5%)
    psum x1, waiting for transfers between devices, on_device(): lax.psum((grad_first, grad_second), ('graph', 'dom'))  112 us
    all_to_all x1, blocking collectives, on_device(): lax.all_to_all(grad_arrived.reshape(devices, slot_cap, feat_width), ('gra...  41.7 us
    all_to_all x1, waiting for transfers between devices, on_device(): lax.all_to_all(outgoing, ('graph', 'dom'), split_axis=0, concat_axis=0, t...  36.7 us
    ppermute x4, starting transfers between devices, with_halo(): lax.ppermute(head, axis, [((i + 1) % count, i) for i in range(count)])  20.9 us
    unnamed x64, local copies, waits for them, and re-layouts  8.23 us
    dot_general x4, matrix products, aggregate(): jnp.dot(counts, pool, precision=TOP_PRECISION, preferred_element_type=jnp...  8.09 us
    scatter-add x1, other arithmetic, on_device(): jnp.zeros((row_count + 1, feat_width), jnp.float32).at[routes].add(returned)  7.75 us
    ppermute x4, waiting for transfers between devices, with_halo(): lax.ppermute(tail, axis, [(i, (i + 1) % count) for i in range(count)])  7.13 us
  transfers between devices with their start and end apart: 10, of which 5 were waited for; matrix products, arithmetic and copies ran while one was open for 6% of the time, Pallas kernels for 0%

commit v1 on v0

v1 whole, which is shorter than its diff:
```python
import functools
import math

import jax
import jax.numpy as jnp
from jax import lax
from jax.experimental import pallas as pl
from jax.experimental.pallas import tpu as pltpu
from jax.sharding import PartitionSpec as P

HEAT = 1.0 / 0.02
EPSILON = 1e-06
F32 = jnp.float32
BF16 = jnp.bfloat16
MESH = pl.DeviceIdType.MESH


def pieces(x):
    high = x.astype(BF16)
    return high, (x - high.astype(F32)).astype(BF16)


def mm(a, b, ca=1, cb=0):
    return lax.dot_general(a, b, (((ca,), (cb,)), ((), ())), preferred_element_type=F32)


def mm2(exact, x, ca=1, cb=0):
    high, low = pieces(x)
    return mm(exact, high, ca, cb) + mm(exact, low, ca, cb)


def mm3(a, b, ca=1, cb=0):
    ah, al = pieces(a)
    bh, bl = pieces(b)
    return mm(ah, bh, ca, cb) + (mm(ah, bl, ca, cb) + mm(al, bh, ca, cb))


def one_hot(ids, shape, axis):
    return (ids == lax.broadcasted_iota(jnp.int32, shape, axis)).astype(F32).astype(BF16)


def kernel(
    sizes,
    emb_ref,
    w1_ref,
    w2_ref,
    nb_ref,
    cols_ref,
    rows_ref,
    gemb_ref,
    g1_ref,
    g2_ref,
    loss_ref,
    x_s,
    w1_s,
    w2_s,
    adj,
    mix1,
    mix2,
    hid,
    unit_s,
    out1,
    in1,
    out2,
    in2,
    rec,
    hs,
    hr,
    pk,
    pair_in,
    half_s,
    rs_in,
    red,
    fin,
    halo_ss,
    halo_rs,
    a_ss,
    a_rs,
    pair_ss,
    pair_rs,
    rs_ss,
    rs_rs,
    ag_ss,
    ag_rs,
    back_ss,
    back_rs,
):
    n_graph, n_dom, cap, feat, rows, rim, n_pair = sizes
    n_dev = n_graph * n_dom
    slots = n_dev * cap
    half = slots // 2
    wide = x_s.shape[1]
    part = in1.shape[1] - 2 * cap
    packed = part != cap
    my_g = lax.axis_index("graph")
    my_d = lax.axis_index("dom")
    me = my_g * n_dom + my_d
    other = 1 - my_g
    below = lax.rem(my_d + n_dom - 1, n_dom)
    above = lax.rem(my_d + 1, n_dom)

    barrier = pltpu.get_barrier_semaphore()

    def greet(k, carry):
        o = lax.rem(me + k, n_dev)
        pl.semaphore_signal(
            barrier, inc=1, device_id=(o // n_dom, lax.rem(o, n_dom)), device_id_type=MESH
        )
        return carry

    lax.fori_loop(1, n_dev, greet, 0)

    def remote(src, dst, ss, rs, device):
        return pltpu.make_async_remote_copy(
            src_ref=src, dst_ref=dst, send_sem=ss, recv_sem=rs, device_id=device, device_id_type=MESH
        )

    def halo(p):
        return (
            remote(hs.at[p, 0], hr.at[p, 1], halo_ss.at[p, 0], halo_rs.at[p, 1], (my_g, below)),
            remote(hs.at[p, 1], hr.at[p, 0], halo_ss.at[p, 1], halo_rs.at[p, 0], (my_g, above)),
        )

    def send_halo(p, edge):
        hs[p] = edge.reshape(2, rim, wide)
        for copy in halo(p):
            copy.start()

    def take_halo(p):
        for copy in halo(p):
            copy.wait()
        return hr[p].reshape(2 * rim, wide)

    x_s[...] = jnp.zeros_like(x_s)
    x_s[:, 0:feat] = emb_ref[...]
    x = x_s[...]
    bsel = one_hot(cols_ref[0 : 2 * rim, 1:2], (2 * rim, rows), 1)
    edge = mm2(bsel, x)
    pl.semaphore_wait(barrier, n_dev - 1)
    send_halo(0, edge)

    for dst, src in ((w1_s, w1_ref), (w2_s, w2_ref)):
        dst[...] = jnp.zeros_like(dst)
        dst[0:feat, 0:feat] = src[...]

    block = 32

    def build(i, carry):
        at = pl.multiple_of(i * block, block)
        c = lax.broadcasted_iota(jnp.int32, (block, rows + 2 * rim), 1)
        r = lax.broadcasted_iota(jnp.int32, (block, rows + 2 * rim), 0) + at
        ids = jnp.where(c < rows, c + rim, jnp.where(c < rows + rim, c - rows, c))
        nb = nb_ref[pl.ds(at, block), :]
        deg = cols_ref[pl.ds(at, block), 3:4]
        k = lax.broadcasted_iota(jnp.int32, nb.shape, 1)
        nb = jnp.where(k < deg, nb, -1)
        total = jnp.where(c == r, 1.0, 0.0)
        for j in range(nb.shape[1]):
            total = total + jnp.where(nb[:, j : j + 1] == ids, 1.0, 0.0)
        adj[pl.ds(at, block), :] = total.astype(BF16)
        return carry

    lax.fori_loop(0, rows // block, build, 0)
    inv = 1.0 / (1.0 + cols_ref[0:rows, 3:4].astype(F32))

    own = mm2(adj[:, 0:rows], x)
    mix1[...] = (own + mm2(adj[:, rows:], take_halo(0))) * inv
    hid[...] = jnp.tanh(mm3(mix1[...], w1_s[...]))
    hidden = hid[...]
    send_halo(1, mm2(bsel, hidden))
    own = mm2(adj[:, 0:rows], hidden)
    mix2[...] = (own + mm2(adj[:, rows:], take_halo(1))) * inv
    latent = mm3(mix2[...], w2_s[...])
    inv_len = 1.0 / jnp.sqrt(jnp.sum(latent * latent, axis=1, keepdims=True) + EPSILON)
    unit_s[...] = latent * inv_len

    def put(ref, m, first):
        count = m.shape[0] // cap
        ref[first : first + count, 0:cap, :] = m[:, 0:128].reshape(count, cap, 128)
        ref[first : first + count, cap : 2 * cap, :] = m[:, 128:256].reshape(count, cap, 128)
        last = m[:, 256:384].reshape(count, cap, 128)
        if packed:
            late = pltpu.roll(last[:, part:].reshape(count * part, 128), 64, 1)
            last = last[:, 0:part] + late.reshape(count, part, 128)
        ref[first : first + count, 2 * cap :, :] = last

    def get(ref, dst):
        dst[:, 0:128] = ref[:, 0:cap, :].reshape(slots, 128)
        dst[:, 128:256] = ref[:, cap : 2 * cap, :].reshape(slots, 128)
        last = ref[:, 2 * cap :, :]
        if packed:
            flat = last.reshape(n_dev * part, 128)
            keep = lax.broadcasted_iota(jnp.int32, flat.shape, 1) < 64
            early = jnp.where(keep, flat, 0.0).reshape(n_dev, part, 128)
            late = jnp.where(keep, pltpu.roll(flat, 64, 1), 0.0).reshape(n_dev, part, 128)
            last = jnp.concatenate([early, late], axis=1)
        dst[:, 256:384] = last.reshape(slots, 128)

    def to_owner(q, src, dst, o, land):
        return remote(
            src.at[o],
            dst.at[land],
            a_ss.at[q, o],
            a_rs.at[q, land],
            (o // n_dom, lax.rem(o, n_dom)),
        )

    def send_part(q, src, dst, graph):
        def step(k, carry):
            d = lax.rem(my_d + k, n_dom)
            o = graph * n_dom + d

            @pl.when(o != me)
            def _():
                to_owner(q, src, dst, o, me).start()

            return carry

        lax.fori_loop(0, n_dom, step, 0)

    def wait_all(q, src, dst):
        def step(k, carry):
            o = lax.rem(me + k, n_dev)
            to_owner(q, src, dst, o, o).wait()
            return carry

        lax.fori_loop(1, n_dev, step, 0)
        dst[pl.ds(me, 1)] = src[pl.ds(me, 1)]

    for graph in range(n_graph):
        lo = graph * half
        route = one_hot(cols_ref[lo : lo + half, 0:1], (half, rows), 1)
        put(out1, mm2(route, unit_s[...]), graph * n_dom)
        send_part(0, out1, in1, graph)

    unroute = one_hot(rows_ref[0:1, :], (rows, slots), 0)
    unbound = one_hot(rows_ref[1:2, 0 : 2 * rim], (rows, 2 * rim), 0)
    pair_a = one_hot(cols_ref[0:n_pair, 2:3], (n_pair, half), 1)
    pair_b = one_hot(cols_ref[n_pair : 2 * n_pair, 2:3] - half, (n_pair, half), 1)
    live = rows_ref[2:3, :].astype(F32)

    wait_all(0, out1, in1)
    get(in1, rec)
    r0 = rec[0:half]
    r1 = rec[half:slots]
    a = mm2(pair_a, r0)
    b = mm2(pair_b, r1)
    e1 = jnp.exp(mm3(a, r1, 1, 1) * HEAT) * live[:, half:]
    e2 = jnp.exp(mm3(b, r0, 1, 1) * HEAT) * live[:, :half]
    t1 = jnp.sum(e1, axis=1, keepdims=True)
    t2 = jnp.sum(e2, axis=1, keepdims=True)
    s1 = e1 * (1.0 / t1)
    s2 = e2 * (1.0 / t2)
    match = jnp.sum(a * b, axis=1, keepdims=True) * HEAT
    loss_ref[...] = jnp.sum(jnp.log(t1) + jnp.log(t2) - 2.0 * match, axis=0, keepdims=True) * (
        1.0 / (2.0 * n_pair)
    )
    da = HEAT * (mm3(s1, r1) - 2.0 * b)
    put(out2, mm3(s2, HEAT * b, 0, 0) + mm2(pair_a, da, 0, 0), 0)
    send_part(1, out2, in2, 0)
    db = HEAT * (mm3(s2, r0) - 2.0 * a)
    put(out2, mm3(s1, HEAT * a, 0, 0) + mm2(pair_b, db, 0, 0), n_dom)
    send_part(1, out2, in2, 1)
    wait_all(1, out2, in2)
    get(in2, rec)

    tall = -(-feat // 16) * 16
    chunk = half_s.shape[2]

    def pack_sum(w, g):
        last = g[0:tall, 256:384]
        last = last[0 : tall // 2] + pltpu.roll(last[tall // 2 :], 64, 1)
        spare = jnp.zeros((n_dev * chunk - 5 * tall // 2, 128), F32)
        flat = jnp.concatenate([g[0:tall, 0:128], g[0:tall, 128:256], last, spare], axis=0)
        pk[w] = flat.reshape(n_graph, n_dom, chunk, 128)

    def pair_copy(w):
        return remote(
            pk.at[w, other], pair_in.at[w], pair_ss.at[w], pair_rs.at[w], (other, my_d)
        )

    def scatter_copy(w, d, land):
        return remote(
            half_s.at[w, d], rs_in.at[w, land], rs_ss.at[w, d], rs_rs.at[w, land], (my_g, d)
        )

    def gather_copy(w, d, land):
        return remote(
            red.at[w], fin.at[w, my_g, land], ag_ss.at[w, d], ag_rs.at[w, land], (my_g, d)
        )

    def each_chip(do):
        def step(k, carry):
            do(lax.rem(my_d + k, n_dom))
            return carry

        lax.fori_loop(1, n_dom, step, 0)

    def sum_scatter(w):
        pair_copy(w).wait()
        half_s[w] = pk[w, pl.ds(my_g, 1)].reshape(n_dom, chunk, 128) + pair_in[w]
        each_chip(lambda d: scatter_copy(w, d, my_d).start())

    def sum_gather(w):
        each_chip(lambda d: scatter_copy(w, d, d).wait())
        rs_in[w, pl.ds(my_d, 1)] = half_s[w, pl.ds(my_d, 1)]
        total = jnp.sum(rs_in[w], axis=0) * (1.0 / math.sqrt(rows * n_dev))
        red[w] = total
        fin[w, pl.ds(my_g, 1), pl.ds(my_d, 1)] = total.reshape(1, 1, chunk, 128)
        each_chip(lambda d: gather_copy(w, d, my_d).start())

    def back_copy(w, side):
        return remote(
            fin.at[w, my_g], fin.at[w, side], back_ss.at[w], back_rs.at[w], (other, my_d)
        )

    def sum_back(w):
        each_chip(lambda d: gather_copy(w, d, d).wait())
        back_copy(w, my_g).start()

    def sum_end(w, ref):
        back_copy(w, my_g).wait_send()
        back_copy(w, other).wait_recv()
        flat = fin[w].reshape(n_dev * chunk, 128)
        ref[:, 0:128] = flat[0:feat]
        ref[:, 128:256] = flat[tall : tall + feat]
        last = flat[2 * tall : 2 * tall + tall // 2]
        last = jnp.concatenate([last, pltpu.roll(last, 64, 1)], axis=0)
        ref[:, 256:feat] = last[0:feat, 0 : feat - 256]

    unit = unit_s[...]
    grad_unit = mm2(unroute, rec[...])
    grad_latent = (
        grad_unit - unit * jnp.sum(grad_unit * unit, axis=1, keepdims=True)
    ) * inv_len
    pack_sum(1, mm3(mix2[...], grad_latent, 0, 0))
    pair_copy(1).start()
    grad_mix = mm3(grad_latent, w2_s[...], 1, 1) * inv
    send_halo(2, mm2(adj[:, rows:], grad_mix, 0, 0))
    own = mm2(adj[:, 0:rows], grad_mix, 0, 0)
    sum_scatter(1)
    grad_hidden = own + mm2(unbound, take_halo(2))
    hidden = hid[...]
    grad_inner = grad_hidden * (1.0 - hidden * hidden)
    pack_sum(0, mm3(mix1[...], grad_inner, 0, 0))
    pair_copy(0).start()
    grad_mix = mm3(grad_inner, w1_s[...], 1, 1) * inv
    sum_scatter(0)
    sum_gather(1)
    send_halo(3, mm2(adj[:, rows:], grad_mix, 0, 0))
    own = mm2(adj[:, 0:rows], grad_mix, 0, 0)
    sum_gather(0)
    sum_back(1)
    grad_x = own + mm2(unbound, take_halo(3))
    gemb_ref[...] = grad_x[:, 0:feat]
    sum_end(1, g2_ref)
    sum_back(0)
    sum_end(0, g1_ref)


def on_device(
    embeddings,
    first_weight,
    second_weight,
    bound_index,
    neighbors,
    degree,
    send_index,
    recv_count,
    pair_index,
):
    rows, feat = embeddings.shape[1:]
    rim = bound_index.shape[-1]
    n_graph = lax.axis_size("graph")
    n_dom = lax.axis_size("dom")
    n_dev = n_graph * n_dom
    cap = send_index.shape[-1]
    n_pair = pair_index.shape[-1]
    slots = n_dev * cap
    wide = -(-feat // 128) * 128
    pool = rows + 2 * rim

    live = jnp.arange(cap, dtype=jnp.int32)[None, :] < recv_count[0, 0][:, None]

    def line(v):
        v = v.reshape(-1)
        return jnp.pad(v, (0, slots - v.shape[0]))

    table = jnp.stack(
        [
            line(send_index),
            line(bound_index),
            line(pair_index),
            line(degree),
        ]
    )
    rows_in = jnp.stack(
        [
            line(send_index),
            line(bound_index),
            line(live.astype(jnp.int32)),
        ]
    )

    part = cap // 2 if cap % 16 == 0 else cap
    tall = -(-feat // 16) * 16
    chunk = -(-(5 * tall // 2) // (8 * n_dev)) * 8
    sem = pltpu.SemaphoreType.DMA
    vmem = pltpu.VMEM
    sizes = (n_graph, n_dom, cap, feat, rows, rim, n_pair)
    grad_emb, g1, g2, loss = pl.pallas_call(
        functools.partial(kernel, sizes),
        out_shape=(
            jax.ShapeDtypeStruct((rows, feat), F32),
            jax.ShapeDtypeStruct((feat, feat), F32),
            jax.ShapeDtypeStruct((feat, feat), F32),
            jax.ShapeDtypeStruct((1, 1), F32),
        ),
        in_specs=[pl.BlockSpec(memory_space=pltpu.VMEM)] * 6,
        out_specs=[pl.BlockSpec(memory_space=pltpu.VMEM)] * 4,
        scratch_shapes=[
            vmem((rows, wide), F32),
            vmem((wide, wide), F32),
            vmem((wide, wide), F32),
            vmem((rows, pool), BF16),
            vmem((rows, wide), F32),
            vmem((rows, wide), F32),
            vmem((rows, wide), F32),
            vmem((rows, wide), F32),
            vmem((n_dev, 2 * cap + part, 128), F32),
            vmem((n_dev, 2 * cap + part, 128), F32),
            vmem((n_dev, 2 * cap + part, 128), F32),
            vmem((n_dev, 2 * cap + part, 128), F32),
            vmem((slots, wide), F32),
            vmem((4, 2, rim, wide), F32),
            vmem((4, 2, rim, wide), F32),
            vmem((2, n_graph, n_dom, chunk, 128), F32),
            vmem((2, n_dom, chunk, 128), F32),
            vmem((2, n_dom, chunk, 128), F32),
            vmem((2, n_dom, chunk, 128), F32),
            vmem((2, chunk, 128), F32),
            vmem((2, n_graph, n_dom, chunk, 128), F32),
            sem((4, 2)),
            sem((4, 2)),
            sem((2, n_dev)),
            sem((2, n_dev)),
            sem((2,)),
            sem((2,)),
            sem((2, n_dom)),
            sem((2, n_dom)),
            sem((2, n_dom)),
            sem((2, n_dom)),
            sem((2,)),
            sem((2,)),
        ],
        compiler_params=pltpu.CompilerParams(
            collective_id=0, has_side_effects=True, vmem_limit_bytes=50 * 1024 * 1024
        ),
    )(embeddings[0], first_weight, second_weight, neighbors[0], table.T, rows_in)
    return grad_emb[None], g1, g2, loss


def solution(mesh):
    in_specs = (
        P("graph", "dom", None),
        P(),
        P(),
        P("graph", "dom", None, None),
        P("graph", "dom", None),
        P("graph", "dom"),
        P("graph", "dom", None, None),
        P("graph", "dom", None),
        P("graph", "dom", None, None),
    )
    out_specs = (P("graph", "dom", None), P(), P(), P("graph", "dom"))
    return jax.shard_map(
        on_device, mesh=mesh, in_specs=in_specs, out_specs=out_specs, check_vma=False
    )
```

time: 332 us -> 127 us (0.38)
  waiting for transfers between devices: 155 us -> 0 us
  Pallas kernels: 0 us -> 115 us
  blocking collectives: 41.7 us -> 0 us
  starting transfers between devices: 30.2 us -> 0 us
  other arithmetic: 30.1 us -> 0.77 us
  matrix products: 26.7 us -> 0 us
  local copies, waits for them, and re-layouts: 30.7 us -> 8.2 us
  between operations: 16.4 us -> 2.47 us
    pallas_call x0 -> x1, Pallas kernels: none -> 115 us  [on_device(): pl.pallas_call(functools.partial(kernel, sizes), out_shape=(jax.ShapeDtyp...]
    psum x1 -> x0, waiting for transfers between devices: 112 us -> none  [on_device(): lax.psum((grad_first, grad_second), ('graph', 'dom'))]
    all_to_all x1 -> x0, blocking collectives: 41.7 us -> none  [on_device(): lax.all_to_all(grad_arrived.reshape(devices, slot_cap, feat_width), ('gra...]
    all_to_all x1 -> x0, waiting for transfers between devices: 36.7 us -> none  [on_device(): lax.all_to_all(outgoing, ('graph', 'dom'), split_axis=0, concat_axis=0, t...]
    dot_general x16 -> x0, matrix products: 26.7 us -> none  [the longest x4 8.09 us: aggregate(): jnp.dot(counts, pool, precision=TOP_PRECISION, preferred_element_type=jnp...]
    ppermute x8 -> x0, starting transfers between devices: 24.1 us -> none  [the longest x4 20.9 us: with_halo(): lax.ppermute(head, axis, [((i + 1) % count, i) for i in range(count)])]
    scatter-add x5 -> x0, other arithmetic: 12.9 us -> none  [the longest x1 7.75 us: on_device(): jnp.zeros((row_count + 1, feat_width), jnp.float32).at[routes].add(returned)]
    gather x11 -> x0, local copies, waits for them, and re-layouts: 12.5 us -> none  [the longest x1 4.83 us: on_device(): outgoing = padded[routes]]
  transfers between devices with their start and end apart: 10 -> 0, of which waited for: 5 -> 0; matrix products, arithmetic and copies ran while one was open for 6% -> 0% of each run, Pallas kernels for 0% -> 0%
where the time goes in v1:
time: 127 us; the launch traced here: 126 us
  Pallas kernels  115 us (91%)
  local copies, waits for them, and re-layouts  8.2 us (6%)
  between operations  2.47 us (2%)
    pallas_call x1, Pallas kernels, on_device(): pl.pallas_call(functools.partial(kernel, sizes), out_shape=(jax.ShapeDtyp...  115 us
    unnamed x11, local copies, waits for them, and re-layouts  4.9 us

profile of v1, /device:TPU:0, one launch (start us, length us, event | category | flops | bytes accessed | tf_op | source)
XLA Modules:
  0.0 126.5 jit_solution(13769003643724691341)
XLA Ops:
  0.6 0.0 copy-start.2
  0.6 0.8 reshape.51
  1.5 0.8 stack.21
  2.3 0.7 pad.15
  3.0 0.7 pad.14
  3.7 0.7 fusion
  4.4 0.1 reshape.54
  4.5 0.9 copy.14
  5.4 0.2 copy.15.cols_ref
  5.6 0.0 copy-done.2
  5.6 0.0 copy-start
  5.6 0.0 copy-start.1
  5.6 1.3 %copy.13 = f32[1,512,300]{2,1,0:T(8,128)} copy(f32[1,512,300]{1,0,2:T(1,128)S(1)} %copy-done.2) | data formatting | bytes 1228800 | tf_op args[0]
  7.0 0.0 copy-done
  7.0 0.0 copy-done.1
  7.0 115.1 %shard_map.120 = (f32[512,300]{1,0:T(8,128)S(1)}, f32[300,300]{1,0:T(8,128)S(1)}, f32[300,300]{1,0:T(8,128)S(1)}, f32[1,1]{1,0:T(1,128)}) custom-call(f32[512,300]{1,0:T(8,128)} %bitcast.15, f32[300,300]{1,0:T(8,128)S(1)} %copy-done, f32[300,300]{1,0:T(8,128)S(1)} %copy-done.1, s32[512,16]{1,0:T(8,128)S(1)} %bitcast.13, s32[1024,4]{1,0:T(8,128)S(1)} %copy.15.cols_ref, ...), custom_call_target="tpu_custom_call" | custom-call | tf_op jit(solution)/shard_map/pallas_call | solution.py:411
  122.1 1.1 copy.16
  123.2 0.8 copy.20
  124.0 0.8 copy.21
  (3 shorter events, 0.0 us)
Async XLA Ops:
  0.6 5.0 %copy-start.2 = (f32[1,512,300]{1,0,2:T(1,128)S(1)}, f32[1,512,300]{1,0,2:T(1,128)}, u32[]{:S(2)}) copy-start(f32[1,512,300]{1,0,2:T(1,128)} %param.9) | copy-start | bytes 1843204
  5.6 1.4 %copy-start = (f32[300,300]{1,0:T(8,128)S(1)}, f32[300,300]{1,0:T(8,128)}, u32[]{:S(2)}) copy-start(f32[300,300]{1,0:T(8,128)} %w1_ref.1) | copy-start | bytes 1080004
  5.6 1.4 %copy-start.1 = (f32[300,300]{1,0:T(8,128)S(1)}, f32[300,300]{1,0:T(8,128)}, u32[]{:S(2)}) copy-start(f32[300,300]{1,0:T(8,128)} %w2_ref.1) | copy-start | bytes 1080004

commit v2 on v1

--- a/solution.py
+++ b/solution.py
@@ -24,15 +24,22 @@
     return lax.dot_general(a, b, (((ca,), (cb,)), ((), ())), preferred_element_type=F32)
 
 
+def both(x, axis=1):
+    return jnp.concatenate(pieces(x), axis=axis)
+
+
 def mm2(exact, x, ca=1, cb=0):
-    high, low = pieces(x)
-    return mm(exact, high, ca, cb) + mm(exact, low, ca, cb)
+    width = x.shape[1 - cb]
+    full = mm(exact, both(x, 1 - cb), ca, cb)
+    return full[:, 0:width] + full[:, width:]
 
 
 def mm3(a, b, ca=1, cb=0):
     ah, al = pieces(a)
     bh, bl = pieces(b)
-    return mm(ah, bh, ca, cb) + (mm(ah, bl, ca, cb) + mm(al, bh, ca, cb))
+    width = b.shape[1 - cb]
+    full = mm(ah, jnp.concatenate([bh, bl], axis=1 - cb), ca, cb)
+    return full[:, 0:width] + (full[:, width:] + mm(al, bh, ca, cb))
 
 
 def one_hot(ids, shape, axis):
@@ -45,8 +52,11 @@
     w1_ref,
     w2_ref,
     nb_ref,
-    cols_ref,
-    rows_ref,
+    deg_ref,
+    send_ref,
+    bound_ref,
+    count_ref,
+    pairs_ref,
     gemb_ref,
     g1_ref,
     g2_ref,
@@ -54,7 +64,10 @@
     x_s,
     w1_s,
     w2_s,
+    ids_s,
+    cols_s,
     adj,
+    adj_t,
     mix1,
     mix2,
     hid,
@@ -134,7 +147,14 @@
     x_s[...] = jnp.zeros_like(x_s)
     x_s[:, 0:feat] = emb_ref[...]
     x = x_s[...]
-    bsel = one_hot(cols_ref[0 : 2 * rim, 1:2], (2 * rim, rows), 1)
+    ids_s[...] = jnp.zeros_like(ids_s)
+    ids_s[0:1, :] = send_ref[...]
+    ids_s[1:2, 0 : 2 * rim] = bound_ref[...]
+    ids_s[2:3, 0:n_pair] = pairs_ref[0:1, :]
+    ids_s[2:3, n_pair : 2 * n_pair] = pairs_ref[1:2, :]
+    ids_s[3:4, 0:rows] = deg_ref[...]
+    cols_s[...] = jnp.transpose(ids_s[...].astype(F32)).astype(jnp.int32)
+    bsel = one_hot(cols_s[0 : 2 * rim, 1:2], (2 * rim, rows), 1)
     edge = mm2(bsel, x)
     pl.semaphore_wait(barrier, n_dev - 1)
     send_halo(0, edge)
@@ -144,31 +164,31 @@
         dst[0:feat, 0:feat] = src[...]
 
     block = 32
+    slot = lax.broadcasted_iota(jnp.int32, nb_ref.shape, 0)
+    near = jnp.where(slot < deg_ref[...], nb_ref[...], -1)
 
     def build(i, carry):
         at = pl.multiple_of(i * block, block)
-        c = lax.broadcasted_iota(jnp.int32, (block, rows + 2 * rim), 1)
-        r = lax.broadcasted_iota(jnp.int32, (block, rows + 2 * rim), 0) + at
-        ids = jnp.where(c < rows, c + rim, jnp.where(c < rows + rim, c - rows, c))
-        nb = nb_ref[pl.ds(at, block), :]
-        deg = cols_ref[pl.ds(at, block), 3:4]
-        k = lax.broadcasted_iota(jnp.int32, nb.shape, 1)
-        nb = jnp.where(k < deg, nb, -1)
-        total = jnp.where(c == r, 1.0, 0.0)
-        for j in range(nb.shape[1]):
-            total = total + jnp.where(nb[:, j : j + 1] == ids, 1.0, 0.0)
-        adj[pl.ds(at, block), :] = total.astype(BF16)
+        p = lax.broadcasted_iota(jnp.int32, (block, rows), 0) + at
+        r = lax.broadcasted_iota(jnp.int32, (block, rows), 1)
+        ids = jnp.where(p < rows, p + rim, jnp.where(p < rows + rim, p - rows, p))
+        total = jnp.where(p == r, 1.0, 0.0)
+        for j in range(near.shape[0]):
+            total = total + jnp.where(near[j : j + 1, :] == ids, 1.0, 0.0)
+        adj_t[pl.ds(at, block), :] = total.astype(BF16)
         return carry
 
-    lax.fori_loop(0, rows // block, build, 0)
-    inv = 1.0 / (1.0 + cols_ref[0:rows, 3:4].astype(F32))
+    lax.fori_loop(0, (rows + 2 * rim) // block, build, 0)
+    for at in range(0, rows + 2 * rim, 128):
+        turned = jnp.transpose(adj_t[at : at + 128, :].astype(F32))
+        adj[:, at : at + 128] = turned.astype(BF16)
+    inv = 1.0 / (1.0 + cols_s[0:rows, 3:4].astype(F32))
 
     own = mm2(adj[:, 0:rows], x)
     mix1[...] = (own + mm2(adj[:, rows:], take_halo(0))) * inv
+    send_halo(1, jnp.tanh(mm3(mm2(bsel, mix1[...]), w1_s[...])))
     hid[...] = jnp.tanh(mm3(mix1[...], w1_s[...]))
-    hidden = hid[...]
-    send_halo(1, mm2(bsel, hidden))
-    own = mm2(adj[:, 0:rows], hidden)
+    own = mm2(adj[:, 0:rows], hid[...])
     mix2[...] = (own + mm2(adj[:, rows:], take_halo(1))) * inv
     latent = mm3(mix2[...], w2_s[...])
     inv_len = 1.0 / jnp.sqrt(jnp.sum(latent * latent, axis=1, keepdims=True) + EPSILON)
@@ -229,15 +249,18 @@
 
     for graph in range(n_graph):
         lo = graph * half
-        route = one_hot(cols_ref[lo : lo + half, 0:1], (half, rows), 1)
+        route = one_hot(cols_s[lo : lo + half, 0:1], (half, rows), 1)
         put(out1, mm2(route, unit_s[...]), graph * n_dom)
         send_part(0, out1, in1, graph)
 
-    unroute = one_hot(rows_ref[0:1, :], (rows, slots), 0)
-    unbound = one_hot(rows_ref[1:2, 0 : 2 * rim], (rows, 2 * rim), 0)
-    pair_a = one_hot(cols_ref[0:n_pair, 2:3], (n_pair, half), 1)
-    pair_b = one_hot(cols_ref[n_pair : 2 * n_pair, 2:3] - half, (n_pair, half), 1)
-    live = rows_ref[2:3, :].astype(F32)
+    unroute = one_hot(ids_s[0:1, :], (rows, slots), 0)
+    unbound = one_hot(ids_s[1:2, 0 : 2 * rim], (rows, 2 * rim), 0)
+    pair_a = one_hot(cols_s[0:n_pair, 2:3], (n_pair, half), 1)
+    pair_b = one_hot(cols_s[n_pair : 2 * n_pair, 2:3] - half, (n_pair, half), 1)
+    source = lax.broadcasted_iota(jnp.int32, (n_dev, slots), 0)
+    place = lax.broadcasted_iota(jnp.int32, (n_dev, slots), 1) - source * cap
+    inside = jnp.where((place >= 0) & (place < count_ref[...]), 1.0, 0.0)
+    live = jnp.sum(inside, axis=0, keepdims=True)
 
     wait_all(0, out1, in1)
     get(in1, rec)
@@ -333,24 +356,24 @@
     grad_latent = (
         grad_unit - unit * jnp.sum(grad_unit * unit, axis=1, keepdims=True)
     ) * inv_len
+    shared = grad_latent * inv
+    send_halo(2, mm3(mm2(adj_t[rows:, :], shared), w2_s[...], 1, 1))
     pack_sum(1, mm3(mix2[...], grad_latent, 0, 0))
     pair_copy(1).start()
-    grad_mix = mm3(grad_latent, w2_s[...], 1, 1) * inv
-    send_halo(2, mm2(adj[:, rows:], grad_mix, 0, 0))
-    own = mm2(adj[:, 0:rows], grad_mix, 0, 0)
+    own = mm2(adj_t[0:rows, :], mm3(shared, w2_s[...], 1, 1))
     sum_scatter(1)
     grad_hidden = own + mm2(unbound, take_halo(2))
     hidden = hid[...]
     grad_inner = grad_hidden * (1.0 - hidden * hidden)
     pack_sum(0, mm3(mix1[...], grad_inner, 0, 0))
     pair_copy(0).start()
-    grad_mix = mm3(grad_inner, w1_s[...], 1, 1) * inv
+    shared = grad_inner * inv
+    send_halo(3, mm3(mm2(adj_t[rows:, :], shared), w1_s[...], 1, 1))
+    sum_gather(1)
     sum_scatter(0)
-    sum_gather(1)
-    send_halo(3, mm2(adj[:, rows:], grad_mix, 0, 0))
-    own = mm2(adj[:, 0:rows], grad_mix, 0, 0)
+    own = mm2(adj_t[0:rows, :], mm3(shared, w1_s[...], 1, 1))
+    sum_back(1)
     sum_gather(0)
-    sum_back(1)
     grad_x = own + mm2(unbound, take_halo(3))
     gemb_ref[...] = grad_x[:, 0:feat]
     sum_end(1, g2_ref)
@@ -380,28 +403,6 @@
     wide = -(-feat // 128) * 128
     pool = rows + 2 * rim
 
-    live = jnp.arange(cap, dtype=jnp.int32)[None, :] < recv_count[0, 0][:, None]
-
-    def line(v):
-        v = v.reshape(-1)
-        return jnp.pad(v, (0, slots - v.shape[0]))
-
-    table = jnp.stack(
-        [
-            line(send_index),
-            line(bound_index),
-            line(pair_index),
-            line(degree),
-        ]
-    )
-    rows_in = jnp.stack(
-        [
-            line(send_index),
-            line(bound_index),
-            line(live.astype(jnp.int32)),
-        ]
-    )
-
     part = cap // 2 if cap % 16 == 0 else cap
     tall = -(-feat // 16) * 16
     chunk = -(-(5 * tall // 2) // (8 * n_dev)) * 8
@@ -416,13 +417,16 @@
             jax.ShapeDtypeStruct((feat, feat), F32),
             jax.ShapeDtypeStruct((1, 1), F32),
         ),
-        in_specs=[pl.BlockSpec(memory_space=pltpu.VMEM)] * 6,
+        in_specs=[pl.BlockSpec(memory_space=pltpu.VMEM)] * 9,
         out_specs=[pl.BlockSpec(memory_space=pltpu.VMEM)] * 4,
         scratch_shapes=[
             vmem((rows, wide), F32),
             vmem((wide, wide), F32),
             vmem((wide, wide), F32),
+            vmem((8, slots), jnp.int32),
+            vmem((slots, 8), jnp.int32),
             vmem((rows, pool), BF16),
+            vmem((pool, rows), BF16),
             vmem((rows, wide), F32),
             vmem((rows, wide), F32),
             vmem((rows, wide), F32),
@@ -456,7 +460,17 @@
         compiler_params=pltpu.CompilerParams(
             collective_id=0, has_side_effects=True, vmem_limit_bytes=50 * 1024 * 1024
         ),
-    )(embeddings[0], first_weight, second_weight, neighbors[0], table.T, rows_in)
+    )(
+        embeddings[0],
+        first_weight,
+        second_weight,
+        neighbors[0].T,
+        degree,
+        send_index.reshape(1, slots),
+        bound_index.reshape(1, 2 * rim),
+        recv_count.reshape(n_dev, 1),
+        pair_index[0, 0],
+    )
     return grad_emb[None], g1, g2, loss
 
 

time: 127 us -> 120 us (0.945)
  Pallas kernels: 115 us -> 111 us
  local copies, waits for them, and re-layouts: 8.2 us -> 6.38 us
    pallas_call x1, Pallas kernels: 115 us -> 111 us  [on_device(): pl.pallas_call(functools.partial(kernel, sizes), out_shape=(jax.ShapeDtyp...]
    pad x3 -> x0, local copies, waits for them, and re-layouts: 1.37 us -> none  [line(): return jnp.pad(v, (0, slots - v.shape[0]))]
    unnamed x11 -> x18, local copies, waits for them, and re-layouts: 4.9 us -> 5.41 us
where the time goes in v2:
time: 120 us
  Pallas kernels  111 us (92%)
  local copies, waits for them, and re-layouts  6.38 us (5%)
  between operations  2.4 us (2%)
    pallas_call x1, Pallas kernels, on_device(): pl.pallas_call(functools.partial(kernel, sizes), out_shape=(jax.ShapeDtyp...  111 us
    unnamed x18, local copies, waits for them, and re-layouts  5.41 us

profile of v2, /device:TPU:0, one launch (start us, length us, event | category | flops | bytes accessed | tf_op | source)
XLA Modules:
  0.0 120.2 jit_solution(10472850321530414537)
XLA Ops:
  0.6 0.0 copy-start.6
  0.6 0.7 copy-done.6
  1.3 0.1 reshape.18.bound_ref
  1.4 0.0 copy-start.5
  1.4 0.8 reshape.17.send_ref
  2.2 0.0 copy-done.5
  2.2 0.1 copy.14.count_ref
  2.3 0.0 copy-start
  2.3 0.0 copy-start.1
  2.3 0.0 copy-start.2
  2.3 0.0 copy-start.3
  2.3 1.4 %copy.13 = f32[1,512,300]{2,1,0:T(8,128)S(1)} copy(f32[1,512,300]{1,0,2:T(1,128)} %param.9) | data formatting | bytes 1228800 | tf_op args[0]
  3.7 0.0 copy-start.4
  3.7 0.0 copy-done
  3.8 0.0 copy-done.1
  3.8 0.0 copy-done.2
  3.8 0.0 copy-done.3
  3.8 0.6 copy-done.4
  4.4 111.4 %shard_map.120 = (f32[512,300]{1,0:T(8,128)S(1)}, f32[300,300]{1,0:T(8,128)S(1)}, f32[300,300]{1,0:T(8,128)S(1)}, f32[1,1]{1,0:T(1,128)}) custom-call(f32[512,300]{1,0:T(8,128)S(1)} %bitcast.9, f32[300,300]{1,0:T(8,128)S(1)} %copy-done, f32[300,300]{1,0:T(8,128)S(1)} %copy-done.1, s32[16,512]{1,0:T(8,128)S(1)} %bitcast.11, s32[1,512]{1,0:T(1,128)S(1)} %copy-done.3, ...), custom_call_target="tpu_custom_call" | custom-call | tf_op jit(solution)/shard_map/pallas_call | solution.py:412
  115.8 1.1 copy.15
  117.0 0.8 copy.19
  117.7 0.8 copy.20
Async XLA Ops:
  0.6 0.7 copy-start.6
  1.4 0.8 copy-start.5
  2.3 1.5 %copy-start = (f32[300,300]{1,0:T(8,128)S(1)}, f32[300,300]{1,0:T(8,128)}, u32[]{:S(2)}) copy-start(f32[300,300]{1,0:T(8,128)} %w1_ref.1) | copy-start | bytes 1080004
  2.3 1.5 %copy-start.1 = (f32[300,300]{1,0:T(8,128)S(1)}, f32[300,300]{1,0:T(8,128)}, u32[]{:S(2)}) copy-start(f32[300,300]{1,0:T(8,128)} %w2_ref.1) | copy-start | bytes 1080004
  2.3 1.5 %copy-start.2 = (s32[1,512,16]{1,2,0:T(8,128)S(1)}, s32[1,512,16]{1,2,0:T(8,128)}, u32[]{:S(2)}) copy-start(s32[1,512,16]{1,2,0:T(8,128)} %param.13) | copy-start | bytes 98308
  2.3 1.5 %copy-start.3 = (s32[1,512]{1,0:T(1,128)S(1)}, s32[1,512]{1,0:T(1,128)}, u32[]{:S(2)}) copy-start(s32[1,512]{1,0:T(1,128)} %deg_ref.1) | copy-start | bytes 6148
  3.7 0.7 copy-start.4
